TPU v7x, 32 devices: a whole 2x2x4 slice. The times are simulated.
32 devices in a mesh: groups: 2 (over x), tensor: 16 (over z, y, core).
Axes of the slice: x: 2, y: 2, z: 4, core: 2. Of those that a mesh axis runs over, the one named last changes fastest.
Arguments:
- tokens: bfloat16 [1024, 8192], P('groups', 'tensor'), parts along dimension 0, may hold values from -6 to 6
- gate_weight: bfloat16 [8192, 14336], P(None, 'tensor'), may hold values from -0.0625 to 0.0625
- up_weight: bfloat16 [8192, 14336], P(None, 'tensor'), may hold values from -0.0625 to 0.0625
- down_weight: bfloat16 [14336, 8192], P('tensor'), may hold values from -0.0625 to 0.0625
- gate_shrink: bfloat16 [8, 8192, 64], P(None, 'tensor'), may hold values from -0.0625 to 0.0625
- gate_expand: bfloat16 [8, 64, 14336], P(None, None, 'tensor'), may hold values from -0.75 to 0.75
- up_shrink: bfloat16 [8, 8192, 64], P(None, 'tensor'), may hold values from -0.0625 to 0.0625
- up_expand: bfloat16 [8, 64, 14336], P(None, None, 'tensor'), may hold values from -0.75 to 0.75
- down_first_factor: bfloat16 [8, 14336, 64], P(None, 'tensor'), may hold values from -0.046875 to 0.046875
- down_expand: bfloat16 [8, 64, 8192], P(None, None, 'tensor'), may hold values from -0.75 to 0.75
- block_adapter: int32 [16], P('groups'), parts along dimension 0, may hold values from 0 to 7, as said below
- live_slot_count: int32 [16], P('groups'), parts along dimension 0, may hold values from 1 to 64, as said below
Outputs:
- mixed: bfloat16 [1024, 8192], P('groups', 'tensor'), parts along dimension 0
There are 2 independent parts, one for each index of `groups`. A program takes and returns all parts, laid end to end along the dimension named above; an argument that names none is the same for every part. Nothing has to cross between parts.
Inputs may be any that keep to these rules, and one draw needn't show every extreme that they name: `live_slot_count`: some block is full in every draw. `block_adapter`: every draw names adapter 0 and adapter 8 - 1 in some blocks.
All inputs are finite; a program needn't handle non-finite values.
Results may differ from a plain program's by a relative error of at most 0.0055.
Values may be sent and summed in bfloat16 or wider, within the bound.
A program may use at most 192 MiB of HBM per device.

v0:
```python
import jax
import jax.numpy as jnp
from jax import lax
from jax.sharding import PartitionSpec as P

SCALE = 0.5


def per_block(left, table, adapter_ids, form):
    return jnp.einsum(form, left, table[adapter_ids], preferred_element_type=jnp.float32)


def local(
    tokens,
    gate_weight,
    up_weight,
    down_weight,
    gate_shrink,
    gate_expand,
    up_shrink,
    up_expand,
    down_first_factor,
    down_expand,
    block_adapter,
    live_slot_count,
):
    token_count, width_dev = tokens.shape
    num_blocks = block_adapter.shape[0]
    row_length = token_count // num_blocks
    ff_dev = gate_weight.shape[1]
    token_row_blocks = tokens.reshape(num_blocks, row_length, width_dev)
    part_gate = per_block(token_row_blocks, gate_shrink, block_adapter, "btd,bdr->btr")
    part_up = per_block(token_row_blocks, up_shrink, block_adapter, "btd,bdr->btr")
    sum_gate, sum_up = lax.psum((part_gate, part_up), "tensor")
    low_gate = sum_gate.astype(jnp.bfloat16)
    low_up = sum_up.astype(jnp.bfloat16)
    columns = lax.all_gather(tokens, "tensor", axis=1, tiled=True)
    gate_sum = jnp.dot(columns, gate_weight, preferred_element_type=jnp.float32)
    up_sum = jnp.dot(columns, up_weight, preferred_element_type=jnp.float32)
    gate_sum = gate_sum + SCALE * per_block(
        low_gate, gate_expand, block_adapter, "btr,brf->btf"
    ).reshape(token_count, ff_dev)
    up_sum = up_sum + SCALE * per_block(low_up, up_expand, block_adapter, "btr,brf->btf").reshape(
        token_count, ff_dev
    )
    hidden_units = (jax.nn.silu(gate_sum) * up_sum).astype(jnp.bfloat16)
    hidden_blocks = hidden_units.reshape(num_blocks, row_length, ff_dev)
    part_down = per_block(hidden_blocks, down_first_factor, block_adapter, "btf,bfr->btr").reshape(
        token_count, -1
    )
    rank_width = part_down.shape[1]
    sum_down = lax.psum(part_down, "tensor")
    base_part = jnp.dot(hidden_units, down_weight, preferred_element_type=jnp.float32)
    own_cols = lax.psum_scatter(base_part, "tensor", scatter_dimension=1, tiled=True)
    adapter_down_term = sum_down.astype(jnp.bfloat16).reshape(num_blocks, row_length, rank_width)
    adapter_term = per_block(adapter_down_term, down_expand, block_adapter, "btr,brd->btd")
    active_rows = (
        lax.broadcasted_iota(jnp.int32, (num_blocks, row_length), 1) < live_slot_count[:, None]
    )
    result = own_cols.reshape(num_blocks, row_length, -1) + SCALE * adapter_term
    return (
        jnp.where(active_rows[:, :, None], result, 0.0)
        .astype(jnp.bfloat16)
        .reshape(token_count, -1)
    )


def solution(mesh):
    placed = (
        P("groups", "tensor"),
        P(None, "tensor"),
        P(None, "tensor"),
        P("tensor", None),
        P(None, "tensor", None),
        P(None, None, "tensor"),
        P(None, "tensor", None),
        P(None, None, "tensor"),
        P(None, "tensor", None),
        P(None, None, "tensor"),
        P("groups"),
        P("groups"),
    )
    return jax.shard_map(
        local, mesh=mesh, in_specs=placed, out_specs=P("groups", "tensor"), check_vma=False
    )
```

profile of v0, /device:TPU:0, one launch (start us, length us, event | category | flops | bytes accessed | tf_op | source)
XLA Modules:
  0.0 325.3 jit_solution(8987403732629604555)
XLA Ops:
  6.5 0.7 all-gather.2.cloned.1.call-update
  7.3 0.7 compare_select_fusion
  8.0 1.6 gather_fusion.2
  9.7 0.3 convolution_bitcast_fusion
  10.0 0.6 gather_fusion
  10.5 0.3 convolution_bitcast_fusion.1
  10.9 0.7 gather_fusion.1
  11.6 0.5 copy-done.7
  12.0 0.7 gather_fusion.3
  12.7 76.5 %all-reduce.3 = (bf16[8,64,64]{2,1,0:T(8,128)(2,1)S(1)}, bf16[8,64,64]{2,1,0:T(8,128)(2,1)S(1)}) all-reduce(f32[8,64,64]{2,1,0:T(8,128)S(1)} %convolution_bitcast_fusion, f32[8,64,64]{2,1,0:T(8,128)S(1)} %convolution_bitcast_fusion.1), channel_id=1, replica_groups=mesh['groups'=2,'tensor'=16] {'tensor'}, use_global_device_ids=true, to_apply=%region_1.0 | all-reduce | flops 65536 | bytes 393216 | tf_op jit(solution)/shard_map/psum | solution.py:34
  89.2 1.7 convolution_multiply_fusion.1
  90.9 1.6 convolution_multiply_fusion
  92.5 3.4 %all-gather.2.cloned.1.call-done = bf16[512,8192]{1,0:T(8,128)(2,1)} async-done(((bf16[512,512]{1,0:T(8,128)(2,1)}), bf16[512,8192]{1,0:T(8,128)(2,1)}) %all-gather.2.cloned.1.call-update) | async-done | bytes 8388624 | tf_op jit(solution)/shard_map/all_gather | solution.py:37
  95.9 14.8 %fusion.7 = f32[512,896]{1,0:T(8,128)} fusion(bf16[512,8192]{1,0:T(8,128)(2,1)} %all-gather.2.cloned.1.call-done, bf16[8192,896]{1,0:T(8,128)(2,1)} %param.13), kind=kOutput, calls=%fused_computation.23 | convolution fusion | flops 7516192768 | bytes 24903680 | tf_op jit(solution)/shard_map/dot_general | solution.py:38
  110.7 15.5 %fusion.1 = bf16[512,896]{1,0:T(8,128)(2,1)S(1)} fusion(f32[8,64,896]{2,1,0:T(8,128)S(1)} %copy-done.6, f32[512,896]{1,0:T(8,128)} %fusion.7, f32[8,64,896]{2,1,0:T(8,128)S(1)} %copy-done.5, bf16[512,8192]{1,0:T(8,128)(2,1)} %all-gather.2.cloned.1.call-done, bf16[8192,896]{1,0:T(8,128)(2,1)} %param.14), kind=kOutput, calls=%fused_computation.8 | convolution fusion | flops 7519862784 | bytes 29491200 | tf_op jit(solution)/shard_map/dot_general | solution.py:39
  126.3 11.5 %fusion.8 = f32[512,8192]{1,0:T(8,128)} fusion(bf16[512,896]{1,0:T(8,128)(2,1)S(1)} %fusion.1, bf16[896,8192]{1,0:T(8,128)(2,1)S(1)} %bitcast.45), kind=kOutput, calls=%fused_computation.24 | convolution fusion | flops 7516192768 | bytes 32374784 | tf_op jit(solution)/shard_map/dot_general | solution.py:53
  137.8 1.2 copy-done.3
  139.0 0.7 gather_fusion.4
  139.7 1.6 gather_fusion.5
  141.3 0.1 iota_compare_fusion
  141.4 0.4 fusion.9
  141.8 65.6 %all-reduce.4 = bf16[512,64]{1,0:T(8,128)(2,1)S(1)} all-reduce(f32[512,64]{1,0:T(8,128)S(1)} %bitcast.41), channel_id=1, replica_groups=mesh['groups'=2,'tensor'=16] {'tensor'}, use_global_device_ids=true, to_apply=%region_3.4 | all-reduce | flops 32768 | bytes 196608 | tf_op jit(solution)/shard_map/psum | solution.py:52
  207.5 108.7 %reduce-scatter.2.cloned.1.call-done = f32[512,512]{1,0:T(8,128)} async-done(((f32[512,8192]{1,0:T(8,128)}), f32[512,512]{1,0:T(8,128)}) %reduce-scatter.2.cloned.1.call-update) | async-done | bytes 1048592 | tf_op jit(solution)/shard_map/reduce_scatter | solution.py:54
  316.2 2.3 fusion.4
  (33 shorter events, 0.1 us)
Async XLA Ops:
  6.5 4.3 %copy-start = (bf16[8,64,896]{2,1,0:T(8,128)(2,1)S(1)}, bf16[8,64,896]{2,1,0:T(8,128)(2,1)}, u32[]{:S(2)}) copy-start(bf16[8,64,896]{2,1,0:T(8,128)(2,1)} %param.17) | copy-start | bytes 2752516
  6.5 3.1 copy-start.2
  6.5 89.4 %all-gather.2.cloned.1.call-start = ((), (), s32[]{:S(2)}) async-start(), calls=%async_computation.1 | async-start | bytes 8912896 | tf_op jit(solution)/shard_map/all_gather | solution.py:37
  7.3 2.7 copy-start.4
  7.3 308.9 %reduce-scatter.2.cloned.1.call-start = ((), (), s32[]{:S(2)}) async-start(), calls=%async_computation.2 | async-start | bytes 17825792 | tf_op jit(solution)/shard_map/reduce_scatter | solution.py:54
  10.8 1.2 copy-start.7
  92.5 18.1 %copy-start.5 = (f32[8,64,896]{2,1,0:T(8,128)S(1)}, f32[8,64,896]{2,1,0:T(8,128)}, u32[]{:S(2)}) copy-start(f32[8,64,896]{2,1,0:T(8,128)} %convolution_multiply_fusion.1) | copy-start | bytes 5505028
  95.9 14.8 %copy-start.6 = (f32[8,64,896]{2,1,0:T(8,128)S(1)}, f32[8,64,896]{2,1,0:T(8,128)}, u32[]{:S(2)}) copy-start(f32[8,64,896]{2,1,0:T(8,128)} %convolution_multiply_fusion) | copy-start | bytes 5505028
  95.9 30.3 %slice-start = ((s8[14680064]{0:T(1024)(128)(4,1)}), s8[4194304]{0:T(1024)(128)(4,1)S(1)}, s32[]{:S(2)}) async-start(s8[14680064]{0:T(1024)(128)(4,1)} %bitcast.44), calls=%async_computation.3 | async-start | bytes 8388608
  95.9 30.3 %slice-start.1 = ((s8[14680064]{0:T(1024)(128)(4,1)}), s8[4194304]{0:T(1024)(128)(4,1)S(1)}, s32[]{:S(2)}) async-start(s8[14680064]{0:T(1024)(128)(4,1)} %bitcast.44), calls=%async_computation.4 | async-start | bytes 8388608
  110.7 15.6 %slice-start.2 = ((s8[14680064]{0:T(1024)(128)(4,1)}), s8[4194304]{0:T(1024)(128)(4,1)S(1)}, s32[]{:S(2)}) async-start(s8[14680064]{0:T(1024)(128)(4,1)} %bitcast.44), calls=%async_computation.5 | async-start | bytes 8388608
  110.7 15.6 %slice-start.3 = ((s8[14680064]{0:T(1024)(128)(4,1)}), s8[2097152]{0:T(1024)(128)(4,1)S(1)}, s32[]{:S(2)}) async-start(s8[14680064]{0:T(1024)(128)(4,1)} %bitcast.44), calls=%async_computation.6 | async-start | bytes 4194304
  126.3 11.5 %copy-start.8 = (bf16[512,896]{1,0:T(8,128)(2,1)}, bf16[512,896]{1,0:T(8,128)(2,1)S(1)}, u32[]{:S(2)}) copy-start(bf16[512,896]{1,0:T(8,128)(2,1)S(1)} %fusion.1) | copy-start | bytes 2752516
  137.8 1.2 copy-start.3
  139.0 2.3 copy-start.10
  139.0 2.4 copy-start.9
  141.4 177.1 %copy-start.1 = (bf16[8,64,896]{2,1,0:T(8,128)(2,1)S(1)}, bf16[8,64,896]{2,1,0:T(8,128)(2,1)}, u32[]{:S(2)}) copy-start(bf16[8,64,896]{2,1,0:T(8,128)(2,1)} %param.17) | copy-start | bytes 2752516
Sparse Core Ops, SparseCore 0:
  9.5 86.3 all-gather.1
  137.9 178.2 reduce-scatter.1
where the time goes:
time: 326 us; the launch traced here: 325 us
  blocking collectives  142 us (44%)
  waiting for transfers between devices  113 us (35%)
  matrix products  48.4 us (15%)
  between operations  13.6 us (4%)
  local copies, waits for them, and re-layouts  7.59 us (2%)
    reduce_scatter x1, waiting for transfers between devices, local(): lax.psum_scatter(base_part, 'tensor', scatter_dimension=1, tiled=True)  109 us
    psum x1, blocking collectives, local(): sum_gate, sum_up = lax.psum((part_gate, part_up), 'tensor')  76.5 us
    psum x1, blocking collectives, local(): sum_down = lax.psum(part_down, 'tensor')  65.6 us
    dot_general x1, matrix products, local(): up_sum = jnp.dot(columns, up_weight, preferred_element_type=jnp.float32)  15.5 us
    dot_general x1, matrix products, local(): gate_sum = jnp.dot(columns, gate_weight, preferred_element_type=jnp.float32)  14.8 us
    dot_general x1, matrix products, local(): jnp.dot(hidden_units, down_weight, preferred_element_type=jnp.float32)  11.5 us
    dot_general x6, matrix products, per_block(): jnp.einsum(form, left, table[adapter_ids], preferred_element_type=jnp.flo...  6.57 us
  transfers between devices with their start and end apart: 2, of which 2 were waited for; matrix products, arithmetic and copies ran while one was open for 3% of the time, Pallas kernels for 0%

commit v1 on v0

--- a/solution.py
+++ b/solution.py
@@ -1,16 +1,453 @@
+import functools
+
 import jax
 import jax.numpy as jnp
 from jax import lax
+from jax.experimental import pallas as pl
+from jax.experimental.pallas import tpu as pltpu
 from jax.sharding import PartitionSpec as P
 
 SCALE = 0.5
+LANES = 128
+F32 = jnp.float32
+BF16 = jnp.bfloat16
+
+
+class Ring:
+    def __init__(self, n):
+        self.n, self.chips = n, n // 2
+        self.half, self.side = self.chips // 2, self.chips // 2
+        self.me = lax.axis_index("tensor")
+        self.chip, self.core = lax.div(self.me, 2), lax.rem(self.me, 2)
+        far, row = lax.div(self.chip, 2), lax.rem(self.chip, 2)
+        self.place = far + row * (2 * self.side - 1 - 2 * far)
+        self.sibling = self.chip * 2 + 1 - self.core
+        self.next = (self.chip_at(1) * 2 + self.core, self.chip_at(-1) * 2 + self.core)
+
+    def chip_at(self, offset):
+        place = lax.rem(self.place + (offset + self.chips), self.chips)
+        row = lax.div(place, self.side)
+        far = place + row * (2 * self.side - 1 - 2 * place)
+        return far * 2 + row
+
+    def peer(self, step):
+        return lax.rem(self.me + step, self.n)
+
+    def sends(self, way, k, h):
+        return k < self.half or (k == self.half and h == way)
+
+
+def greet(ring):
+    barrier = pltpu.get_barrier_semaphore()
+
+    def tell(step, carry):
+        pl.semaphore_signal(barrier, inc=1, device_id={"tensor": ring.peer(step)}, device_id_type=pl.DeviceIdType.MESH)
+        return carry
+
+    lax.fori_loop(1, ring.n, tell, 0)
+    pl.semaphore_wait(barrier, ring.n - 1)
+
+
+def remote(src, dst, send, recv, device):
+    return pltpu.make_async_remote_copy(
+        src_ref=src, dst_ref=dst, send_sem=send, recv_sem=recv,
+        device_id={"tensor": device}, device_id_type=pl.DeviceIdType.MESH,
+    )
+
+
+class Totals:
+    def __init__(self, ring, part, arrived, low, sems):
+        self.ring, self.part, self.arrived, self.low = ring, part, arrived, low
+        self.s1, self.r1, self.s2, self.r2 = sems
+        self.rows = part.shape[0] // ring.n
+
+    def rows_of(self, device):
+        return pl.ds(pl.multiple_of(device * self.rows, self.rows), self.rows)
+
+    def first(self, step):
+        peer = self.ring.peer(step)
+        return remote(self.part.at[self.rows_of(peer)], self.arrived.at[step], self.s1.at[step], self.r1.at[step], peer)
+
+    def second(self, step):
+        rows = self.low.at[self.rows_of(self.ring.me)]
+        return remote(rows, rows, self.s2.at[step], self.r2.at[step], self.ring.peer(step))
+
+    def each(self, do):
+        def body(step, carry):
+            do(step)
+            return carry
+
+        lax.fori_loop(1, self.ring.n, body, 0)
+
+    def scatter(self):
+        self.each(lambda step: self.first(step).start())
+
+    def gather(self):
+        self.each(lambda step: self.first(step).wait_recv())
+        total = self.part[self.rows_of(self.ring.me), :]
+        for step in range(1, self.ring.n):
+            total = total + self.arrived[step]
+        self.low[self.rows_of(self.ring.me), :] = total.astype(BF16)
+        self.each(lambda step: self.second(step).start())
+
+    def finish(self):
+        def wait(step):
+            rows = self.low.at[self.rows_of(self.ring.peer(self.ring.n - step))]
+            remote(rows, rows, self.s2.at[step], self.r2.at[step], self.ring.peer(step)).wait_recv()
+
+        self.each(wait)
+
+    def drain(self):
+        self.each(lambda step: self.first(step).wait_send())
+        self.each(lambda step: self.second(step).wait_send())
+
+
+def gate_up_kernel(
+    n, tok, wg, wu, part, eg, eu, hidden,
+    gath, wbuf, acc, arrived, low,
+    tok_sem, w_sem, ring_send, ring_recv, sib_send, sib_recv, s1, r1, s2, r2,
+):
+    ring = Ring(n)
+    half, chips, core = ring.half, ring.chips, ring.core
+    count, width = tok.shape
+    units = wg.shape[1]
+    hrows = count // 2
+    offsets = [0]
+    for k in range(1, half):
+        offsets += [-k, k]
+    offsets.append(half)
+    slot_of = {offset: slot for slot, offset in enumerate(offsets)}
+
+    def cut(offset, c, h):
+        return gath.at[ring.chip_at(offset), c, pl.ds(h * hrows, hrows)]
+
+    def weight_copies(slot):
+        rows = pl.ds(pl.multiple_of(ring.chip_at(offsets[slot]) * (2 * width), 2 * width), 2 * width)
+        return (
+            pltpu.make_async_copy(wg.at[rows], wbuf.at[slot, :, pl.ds(0, units)], w_sem.at[slot, 0]),
+            pltpu.make_async_copy(wu.at[rows], wbuf.at[slot, :, pl.ds(units, units)], w_sem.at[slot, 1]),
+        )
+
+    def away(way, k):
+        return -k if way == 0 else k
+
+    def pass_on(way, k, h):
+        block = cut(away(way, k - 1), core, h)
+        return remote(block, block, ring_send.at[way, k - 1, h], ring_recv.at[way, k - 1, h], ring.next[way])
+
+    def coming(way, k, h):
+        block = cut(away(way, k), core, h)
+        return remote(block, block, ring_send.at[way, k - 1, h], ring_recv.at[way, k - 1, h], ring.next[way])
+
+    def to_sibling(offset, h, c):
+        block, slot = cut(offset, c, h), slot_of[offset]
+        return remote(block, block, sib_send.at[slot, h], sib_recv.at[slot, h], ring.sibling)
+
+    def relay(k, h):
+        for way in (0, 1):
+            if ring.sends(way, k, h):
+                coming(way, k, h).wait_recv()
+                if ring.sends(way, k + 1, h):
+                    pass_on(way, k + 1, h).start()
+                to_sibling(half if k == half else away(way, k), h, core).start()
+
+    def multiply(offset):
+        slot = slot_of[offset]
+        for copy in weight_copies(slot):
+            copy.wait()
+        for h in (0, 1):
+            to_sibling(offset, h, 1 - core).wait_recv()
+        chip = ring.chip_at(offset)
+
+        def tile(i, carry):
+            lanes = pl.ds(pl.multiple_of(i * 256, 256), 256)
+            new = jnp.dot(gath[chip, 0], wbuf[slot, pl.ds(0, width), lanes], preferred_element_type=F32)
+            new = new + jnp.dot(gath[chip, 1], wbuf[slot, pl.ds(width, width), lanes], preferred_element_type=F32)
+            if slot == 0:
+                acc[:, lanes] = new
+            else:
+                acc[:, lanes] = acc[:, lanes] + new
+            return carry
+
+        lax.fori_loop(0, 2 * units // 256, tile, 0)
+
+    own = pltpu.make_async_copy(tok, gath.at[ring.chip, core], tok_sem)
+    own.start()
+    for slot in range(chips):
+        for copy in weight_copies(slot):
+            copy.start()
+    totals = Totals(ring, part, arrived, low, (s1, r1, s2, r2))
+    greet(ring)
+    own.wait()
+    totals.scatter()
+    for h in (0, 1):
+        for way in (0, 1):
+            pass_on(way, 1, h).start()
+        to_sibling(0, h, core).start()
+    multiply(0)
+    relay(1, 0)
+    totals.gather()
+    relay(1, 1)
+    for k in range(2, half + 1):
+        if k < half:
+            relay(k, 0)
+            multiply(1 - k)
+            relay(k, 1)
+            multiply(k - 1)
+        else:
+            multiply(1 - k)
+            relay(k, 0)
+            relay(k, 1)
+            multiply(k - 1)
+    totals.finish()
+    multiply(half)
+
+    brows = count // eg.shape[0]
+
+    def block(b, carry):
+        rows = pl.ds(pl.multiple_of(b * brows, brows), brows)
+        lowb = low[rows, :]
+        gate = acc[rows, pl.ds(0, units)] + SCALE * jnp.dot(lowb, eg[b], preferred_element_type=F32)
+        up = acc[rows, pl.ds(units, units)] + SCALE * jnp.dot(lowb, eu[b], preferred_element_type=F32)
+        hidden[rows, :] = (gate / (1.0 + jnp.exp(-gate)) * up).astype(BF16)
+        return carry
+
+    lax.fori_loop(0, eg.shape[0], block, 0)
+    totals.drain()
+    for k in range(1, half + 1):
+        for way in (0, 1):
+            for h in (0, 1):
+                if ring.sends(way, k, h):
+                    pass_on(way, k, h).wait_send()
+    for offset in offsets:
+        for h in (0, 1):
+            to_sibling(offset, h, core).wait_send()
+
+
+def down_kernel(
+    n, hidden, wd, first, expand, live, out,
+    wbuf, own, sib_out, sib_in, chain_out, chain_in, part, arrived, low,
+    w_sem, ring_send, ring_recv, sib_send, sib_recv, s1, r1, s2, r2,
+):
+    ring = Ring(n)
+    half, chips, core = ring.half, ring.chips, ring.core
+    count, width = out.shape
+    hrows = count // 2
+    blocks = first.shape[0]
+    brows = count // blocks
+    offsets = [half]
+    for k in range(half - 1, 0, -1):
+        offsets += [k, -k]
+    offsets.append(0)
+    slot_of = {offset: slot for slot, offset in enumerate(offsets)}
+
+    def weight_copy(slot, mine):
+        device = ring.chip_at(offsets[slot]) * 2 + (core if mine == 0 else 1 - core)
+        lanes = pl.ds(pl.multiple_of(device * width, width), width)
+        return pltpu.make_async_copy(wd.at[:, lanes], wbuf.at[slot, mine], w_sem.at[slot, mine])
+
+    def half_rows(h):
+        return pl.ds(h * hrows, hrows)
+
+    def to_sibling(slot):
+        return remote(sib_out.at[slot], sib_in.at[slot], sib_send.at[slot], sib_recv.at[slot], ring.sibling)
+
+    def chain(way, k, h):
+        return remote(
+            chain_out.at[way, k - 1, half_rows(h)], chain_in.at[way, k - 1, half_rows(h)],
+            ring_send.at[way, k - 1, h], ring_recv.at[way, k - 1, h], ring.next[way],
+        )
+
+    def multiply(offset):
+        slot = slot_of[offset]
+        for mine in (1, 0):
+            weight_copy(slot, mine).wait()
+
+            def tile(i, carry):
+                lanes = pl.ds(pl.multiple_of(i * LANES * step, LANES * step), LANES * step)
+                new = jnp.dot(hidden[...], wbuf[slot, mine, :, lanes], preferred_element_type=F32)
+                if mine:
+                    sib_out[slot, :, lanes] = new.astype(BF16)
+                else:
+                    own[slot, :, lanes] = new
+                return carry
+
+            step = 2 if width % 256 == 0 else 1
+            lax.fori_loop(0, width // (LANES * step), tile, 0)
+            if mine:
+                to_sibling(slot).start()
+
+    def send(k, h):
+        for way in (0, 1):
+            if not ring.sends(way, k, h):
+                continue
+            slot = slot_of[half if k == half else (k if way == 0 else -k)]
+            rows = half_rows(h)
+            total = own[slot, rows, :] + sib_in[slot, rows, :].astype(F32)
+            if ring.sends(way, k + 1, h):
+                chain(way, k + 1, h).wait_recv()
+                total = total + chain_in[way, k, rows, :].astype(F32)
+            chain_out[way, k - 1, rows, :] = total.astype(BF16)
+            chain(way, k, h).start()
+
+    def await_sibling(*some):
+        for offset in some:
+            to_sibling(slot_of[offset]).wait_recv()
+
+    for slot in range(chips):
+        for mine in (1, 0):
+            weight_copy(slot, mine).start()
+
+    def shrink(b, carry):
+        rows = pl.ds(pl.multiple_of(b * brows, brows), brows)
+        part[rows, :] = jnp.dot(hidden[rows, :], first[b], preferred_element_type=F32)
+        return carry
+
+    lax.fori_loop(0, blocks, shrink, 0)
+    totals = Totals(ring, part, arrived, low, (s1, r1, s2, r2))
+    greet(ring)
+    multiply(half)
+    totals.scatter()
+    await_sibling(half)
+    send(half, 0)
+    send(half, 1)
+    for k in range(half - 1, 0, -1):
+        multiply(k)
+        multiply(-k)
+        await_sibling(k, -k)
+        if k == half - 1:
+            totals.gather()
+        send(k, 0)
+        if k == 1:
+            multiply(0)
+        send(k, 1)
+    totals.finish()
+    await_sibling(0)
+    last = slot_of[0]
+
+    def join(h):
+        for way in (0, 1):
+            chain(way, 1, h).wait_recv()
+
+        def block(i, carry):
+            b = i + h * (blocks // 2)
+            rows = pl.ds(pl.multiple_of(b * brows, brows), brows)
+            total = own[last, rows, :] + sib_in[last, rows, :].astype(F32)
+            total = total + chain_in[0, 0, rows, :].astype(F32) + chain_in[1, 0, rows, :].astype(F32)
+            total = total + SCALE * jnp.dot(low[rows, :], expand[b], preferred_element_type=F32)
+            out[rows, :] = (total * live[rows, :]).astype(BF16)
+            return carry
+
+        lax.fori_loop(0, blocks // 2, block, 0)
+
+    join(0)
+    join(1)
+    totals.drain()
+    for k in range(1, half + 1):
+        for way in (0, 1):
+            for h in (0, 1):
+                if ring.sends(way, k, h):
+                    chain(way, k, h).wait_send()
+    for slot in range(chips):
+        to_sibling(slot).wait_send()
+
+
+def fused_gate_up(n, tok, wg, wu, part, eg, eu):
+    count, width = tok.shape
+    units = wg.shape[1]
+    chips, half = n // 2, n // 4
+    dma = pltpu.SemaphoreType.DMA
+    return pl.pallas_call(
+        functools.partial(gate_up_kernel, n),
+        out_shape=jax.ShapeDtypeStruct((count, units), BF16),
+        in_specs=[pl.BlockSpec(memory_space=pl.ANY)] * 3 + [pl.BlockSpec(memory_space=pltpu.VMEM)] * 3,
+        out_specs=pl.BlockSpec(memory_space=pltpu.VMEM),
+        scratch_shapes=[
+            pltpu.VMEM((chips, 2, count, width), BF16),
+            pltpu.VMEM((chips, 2 * width, 2 * units), BF16),
+            pltpu.VMEM((count, 2 * units), F32),
+            pltpu.VMEM((n, count // n, LANES), F32),
+            pltpu.VMEM((count, LANES), BF16),
+            dma, dma((chips, 2)), dma((2, half, 2)), dma((2, half, 2)), dma((chips, 2)), dma((chips, 2)),
+            dma((n,)), dma((n,)), dma((n,)), dma((n,)),
+        ],
+        compiler_params=pltpu.CompilerParams(
+            collective_id=0, has_side_effects=True, vmem_limit_bytes=56 * 2**20
+        ),
+        name="gather_gate_up",
+    )(tok, wg, wu, part, eg, eu)
+
+
+def fused_down(n, hidden, wd, first, expand, live):
+    count, units = hidden.shape
+    width = expand.shape[2]
+    chips, half = n // 2, n // 4
+    dma = pltpu.SemaphoreType.DMA
+    return pl.pallas_call(
+        functools.partial(down_kernel, n),
+        out_shape=jax.ShapeDtypeStruct((count, width), BF16),
+        in_specs=[pl.BlockSpec(memory_space=pltpu.VMEM), pl.BlockSpec(memory_space=pl.ANY)]
+        + [pl.BlockSpec(memory_space=pltpu.VMEM)] * 3,
+        out_specs=pl.BlockSpec(memory_space=pltpu.VMEM),
+        scratch_shapes=[
+            pltpu.VMEM((chips, 2, units, width), BF16),
+            pltpu.VMEM((chips, count, width), F32),
+            pltpu.VMEM((chips, count, width), BF16),
+            pltpu.VMEM((chips, count, width), BF16),
+            pltpu.VMEM((2, half, count, width), BF16),
+            pltpu.VMEM((2, half, count, width), BF16),
+            pltpu.VMEM((count, LANES), F32),
+            pltpu.VMEM((n, count // n, LANES), F32),
+            pltpu.VMEM((count, LANES), BF16),
+            dma((chips, 2)), dma((2, half, 2)), dma((2, half, 2)), dma((chips,)), dma((chips,)),
+            dma((n,)), dma((n,)), dma((n,)), dma((n,)),
+        ],
+        compiler_params=pltpu.CompilerParams(
+            collective_id=1, has_side_effects=True, vmem_limit_bytes=56 * 2**20
+        ),
+        name="down_scatter",
+    )(hidden, wd, first, expand, live)
+
+
+def kernel_local(
+    n, tokens, gate_weight, up_weight, down_weight, gate_shrink, gate_expand, up_shrink, up_expand,
+    down_first_factor, down_expand, block_adapter, live_slot_count,
+):
+    count, width = tokens.shape
+    blocks = block_adapter.shape[0]
+    brows = count // blocks
+    rank = gate_shrink.shape[2]
+    held = LANES - rank
+    shrink = jnp.concatenate([gate_shrink[block_adapter], up_shrink[block_adapter]], axis=2)
+    part = jnp.einsum(
+        "btd,bdr->btr", tokens.reshape(blocks, brows, width), shrink, preferred_element_type=F32
+    ).reshape(count, 2 * rank)
+    below, above = ((0, 0), (0, held), (0, 0)), ((0, 0), (held, 0), (0, 0))
+    eg = jnp.pad(gate_expand[block_adapter], below)
+    eu = jnp.pad(up_expand[block_adapter], above)
+    first = jnp.pad(down_first_factor[block_adapter], ((0, 0), (0, 0), (0, held)))
+    expand = jnp.pad(down_expand[block_adapter], below)
+    active = lax.broadcasted_iota(jnp.int32, (blocks, brows), 1) < live_slot_count[:, None]
+    live = active.reshape(count, 1).astype(F32)
+    hidden = fused_gate_up(n, tokens, gate_weight, up_weight, part, eg, eu)
+    return fused_down(n, hidden, down_weight, first, expand, live)
+
+
+def fits(n, tokens, gate_weight, gate_shrink, block_adapter):
+    count, width = tokens.shape
+    units = gate_weight.shape[1]
+    return (
+        n % 4 == 0 and n >= 8 and count % (16 * n) == 0 and width % LANES == 0 and units % LANES == 0
+        and 2 * gate_shrink.shape[2] == LANES and block_adapter.shape[0] % 2 == 0
+        and (count // block_adapter.shape[0]) % 16 == 0
+    )
 
 
 def per_block(left, table, adapter_ids, form):
     return jnp.einsum(form, left, table[adapter_ids], preferred_element_type=jnp.float32)
 
 
-def local(
+def plain_local(
     tokens,
     gate_weight,
     up_weight,
@@ -80,6 +517,13 @@
         P("groups"),
         P("groups"),
     )
+    n = mesh.shape["tensor"]
+
+    def local(*args):
+        if fits(n, args[0], args[1], args[4], args[10]):
+            return kernel_local(n, *args)
+        return plain_local(*args)
+
     return jax.shard_map(
         local, mesh=mesh, in_specs=placed, out_specs=P("groups", "tensor"), check_vma=False
     )

time: 326 us -> 156 us (0.48)
  blocking collectives: 142 us -> 0 us
  Pallas kernels: 0 us -> 134 us
  waiting for transfers between devices: 113 us -> 0 us
  matrix products: 48.4 us -> 2.46 us
  between operations: 13.6 us -> 0.1 us
  local copies, waits for them, and re-layouts: 7.59 us -> 17.5 us
    psum x2 -> x0, blocking collectives: 142 us -> none  [the longest x1 76.5 us: local(): sum_gate, sum_up = lax.psum((part_gate, part_up), 'tensor')]
    pallas_call x0 -> x2, Pallas kernels: none -> 134 us  [the longest x1 75.5 us: fused_gate_up(): pl.pallas_call(functools.partial(gate_up_kernel, n), out_shape=jax.ShapeD...]
    reduce_scatter x1 -> x0, waiting for transfers between devices: 109 us -> none  [local(): lax.psum_scatter(base_part, 'tensor', scatter_dimension=1, tiled=True)]
    dot_general x9 -> x1, matrix products: 48.4 us -> 2.46 us  [kernel_local(): jnp.einsum('btd,bdr->btr', tokens.reshape(blocks, brows, width), shrink,...]
    pad x0 -> x4, local copies, waits for them, and re-layouts: none -> 7.25 us  [the longest x1 3.22 us: kernel_local(): jnp.pad(down_first_factor[block_adapter], ((0, 0), (0, 0), (0, held)))]
    all_gather x1 -> x0, waiting for transfers between devices: 3.36 us -> none  [local(): columns = lax.all_gather(tokens, 'tensor', axis=1, tiled=True)]
    gather x6 -> x9, local copies, waits for them, and re-layouts: 5.91 us -> 7.48 us  [the longest x2 2.36 us: kernel_local(): down_first_factor[block_adapter]]
  transfers between devices with their start and end apart: 2 -> 0, of which waited for: 2 -> 0; matrix products, arithmetic and copies ran while one was open for 3% -> 0% of each run, Pallas kernels for 0% -> 0%
where the time goes in v1:
time: 156 us; the launch traced here: 155 us
  Pallas kernels  134 us (86%)
  local copies, waits for them, and re-layouts  17.5 us (11%)
  matrix products  2.46 us (2%)
    pallas_call x1, Pallas kernels, fused_gate_up(): pl.pallas_call(functools.partial(gate_up_kernel, n), out_shape=jax.ShapeD...  75.5 us
    pallas_call x1, Pallas kernels, fused_down(): pl.pallas_call(functools.partial(down_kernel, n), out_shape=jax.ShapeDtyp...  58.9 us
    pad x1, local copies, waits for them, and re-layouts, kernel_local(): jnp.pad(down_first_factor[block_adapter], ((0, 0), (0, 0), (0, held)))  3.22 us

profile of v1, /device:TPU:0, one launch (start us, length us, event | category | flops | bytes accessed | tf_op | source)
XLA Modules:
  0.0 155.3 jit_solution(9370119678872085710)
XLA Ops:
  0.0 0.0 copy-start
  0.0 0.8 compare_select_fusion
  0.8 1.6 %gather_fusion = bf16[8,512,64]{1,2,0:T(8,128)(2,1)S(1)} fusion(bf16[8,512,64]{1,2,0:T(8,128)(2,1)} %param.16, s32[1024]{0:T(1024)S(1)} %pad_clamp_fusion), kind=kCustom, calls=%fused_computation | custom fusion | bytes 1048608 | tf_op jit(solution)/shard_map/gather | solution.py:421
  2.4 0.5 copy.13
  2.9 0.6 gather_fusion.1
  3.5 0.5 copy.14
  4.0 2.5 %fusion = f32[8,128,64]{1,2,0:T(8,128)} fusion(bf16[8,64,512]{2,1,0:T(8,128)(2,1)} %bitcast.5, bf16[8,512,64]{2,1,0:T(8,128)(2,1)S(1)} %copy.14, bf16[8,512,64]{2,1,0:T(8,128)(2,1)S(1)} %copy.13), kind=kOutput, calls=%fused_computation.6 | convolution fusion | flops 69206016 | bytes 1835008 | tf_op jit(solution)/shard_map/btd,bdr->btr/dot_general | solution.py:422
  6.4 0.0 copy-done
  6.4 0.7 gather_fusion.2
  7.1 1.5 pad.16.eg
  8.6 0.7 gather_fusion.3
  9.3 1.5 pad.17.eu
  10.8 75.5 %gather_gate_up.1.hidden = bf16[512,896]{1,0:T(8,128)(2,1)} custom-call(bf16[512,512]{1,0:T(8,128)(2,1)} %tok.1, bf16[8192,896]{1,0:T(8,128)(2,1)} %wg.1, bf16[8192,896]{1,0:T(8,128)(2,1)} %wu.1, f32[512,128]{1,0:T(8,128)} %bitcast.6, bf16[8,128,896]{2,1,0:T(8,128)(2,1)} %pad.16.eg, bf16[8,128,896]{2,1,0:T(8,128)(2,1)} %pad.17.eu), custom_call_target="tpu_custom_call" | custom-call | tf_op jit(solution)/shard_map/gather_gate_up/pallas_call | solution.py:360
  86.3 0.0 copy-done.1
  86.3 0.7 gather_fusion.4
  87.0 1.7 %copy.15 = bf16[8,896,64]{2,1,0:T(8,128)(2,1)} copy(bf16[8,896,64]{1,2,0:T(8,128)(2,1)S(1)} %gather_fusion.4) | data formatting | bytes 1835008 | tf_op jit(solution)/shard_map/gather | solution.py:428
  88.7 3.2 %pad.18.first = bf16[8,896,128]{2,1,0:T(8,128)(2,1)} pad(bf16[8,896,64]{2,1,0:T(8,128)(2,1)} %copy.15, bf16[]{:T(256)} %constant.6.clone.1), padding=0_0x0_0x0_64 | pad | bytes 2752514 | tf_op jit(solution)/shard_map/jit(_pad)/pad | solution.py:428
  91.9 0.0 copy-done.4
  91.9 0.6 gather_fusion.5
  92.5 1.1 pad.19.expand
  93.6 0.1 fusion.4
  93.6 0.9 reshape.92.live
  94.5 58.9 %down_scatter.1 = bf16[512,512]{1,0:T(8,128)(2,1)} custom-call(bf16[512,896]{1,0:T(8,128)(2,1)} %gather_gate_up.1.hidden, bf16[896,8192]{1,0:T(8,128)(2,1)} %wd.1, bf16[8,896,128]{2,1,0:T(8,128)(2,1)} %pad.18.first, bf16[8,128,512]{2,1,0:T(8,128)(2,1)} %pad.19.expand, f32[512,1]{1,0:T(8,128)} %reshape.92.live), custom_call_target="tpu_custom_call" | custom-call | tf_op jit(solution)/shard_map/down_scatter/pallas_call | solution.py:386
  153.4 1.9 %copy.18 = bf16[512,512]{1,0:T(8,128)(2,1)} copy(bf16[512,512]{1,0:T(8,128)(2,1)} %down_scatter.1) | data formatting | bytes 1048576
  (9 shorter events, 0.0 us)
Async XLA Ops:
  0.0 6.4 %copy-start = (bf16[8,64,896]{2,1,0:T(8,128)(2,1)S(1)}, bf16[8,64,896]{2,1,0:T(8,128)(2,1)}, u32[]{:S(2)}) copy-start(bf16[8,64,896]{2,1,0:T(8,128)(2,1)} %param.17) | copy-start | bytes 2752516
  0.0 2.9 %copy-start.2 = (bf16[8,512,64]{1,2,0:T(8,128)(2,1)S(1)}, bf16[8,512,64]{1,2,0:T(8,128)(2,1)}, u32[]{:S(2)}) copy-start(bf16[8,512,64]{1,2,0:T(8,128)(2,1)} %param.18) | copy-start | bytes 1572868
  6.4 2.2 %copy-start.3 = (bf16[8,64,896]{2,1,0:T(8,128)(2,1)S(1)}, bf16[8,64,896]{2,1,0:T(8,128)(2,1)}, u32[]{:S(2)}) copy-start(bf16[8,64,896]{2,1,0:T(8,128)(2,1)} %param.19) | copy-start | bytes 2752516
  10.8 75.5 %copy-start.1 = (bf16[8,896,64]{1,2,0:T(8,128)(2,1)S(1)}, bf16[8,896,64]{1,2,0:T(8,128)(2,1)}, u32[]{:S(2)}) copy-start(bf16[8,896,64]{1,2,0:T(8,128)(2,1)} %param.20) | copy-start | bytes 2752516
  88.7 3.2 %copy-start.4 = (bf16[8,64,512]{2,1,0:T(8,128)(2,1)S(1)}, bf16[8,64,512]{2,1,0:T(8,128)(2,1)}, u32[]{:S(2)}) copy-start(bf16[8,64,512]{2,1,0:T(8,128)(2,1)} %param.21) | copy-start | bytes 1572868
  91.9 1.7 %copy-start.5 = (s32[8]{0:T(128)S(1)}, s32[8]{0:T(128)}, u32[]{:S(2)}) copy-start(s32[8]{0:T(128)} %param.23) | copy-start | bytes 100

commit v2 on v1

--- a/solution.py
+++ b/solution.py
@@ -55,6 +55,10 @@
     )
 
 
+def across(left, right):
+    return lax.dot_general(left, right, (((1,), (1,)), ((), ())), preferred_element_type=F32)
+
+
 class Totals:
     def __init__(self, ring, part, arrived, low, sems):
         self.ring, self.part, self.arrived, self.low = ring, part, arrived, low
@@ -103,9 +107,9 @@
 
 
 def gate_up_kernel(
-    n, tok, wg, wu, part, eg, eu, hidden,
-    gath, wbuf, acc, arrived, low,
-    tok_sem, w_sem, ring_send, ring_recv, sib_send, sib_recv, s1, r1, s2, r2,
+    n, adapters, tok, wg, wu, gs, us, ge, ue, hidden,
+    gath, wbuf, acc, shrinks, expands, part, arrived, low,
+    tok_sem, table_sem, w_sem, ring_send, ring_recv, sib_send, sib_recv, s1, r1, s2, r2,
 ):
     ring = Ring(n)
     half, chips, core = ring.half, ring.chips, ring.core
@@ -171,19 +175,37 @@
 
         lax.fori_loop(0, 2 * units // 256, tile, 0)
 
+    blocks = adapters.shape[0]
+    brows = count // blocks
     own = pltpu.make_async_copy(tok, gath.at[ring.chip, core], tok_sem)
     own.start()
+    tables = [
+        pltpu.make_async_copy(table, held.at[i], table_sem.at[j])
+        for j, (table, held, i) in enumerate(((gs, shrinks, 0), (us, shrinks, 1), (ge, expands, 0), (ue, expands, 1)))
+    ]
+    for copy in tables:
+        copy.start()
     for slot in range(chips):
         for copy in weight_copies(slot):
             copy.start()
     totals = Totals(ring, part, arrived, low, (s1, r1, s2, r2))
     greet(ring)
     own.wait()
-    totals.scatter()
     for h in (0, 1):
         for way in (0, 1):
             pass_on(way, 1, h).start()
         to_sibling(0, h, core).start()
+    for copy in tables:
+        copy.wait()
+
+    def shrink(b, carry):
+        rows = pl.ds(pl.multiple_of(b * brows, brows), brows)
+        both = jnp.concatenate([shrinks[0, adapters[b]], shrinks[1, adapters[b]]], axis=0)
+        part[rows, :] = across(gath[ring.chip, core, rows, :], both)
+        return carry
+
+    lax.fori_loop(0, blocks, shrink, 0)
+    totals.scatter()
     multiply(0)
     relay(1, 0)
     totals.gather()
@@ -202,17 +224,18 @@
     totals.finish()
     multiply(half)
 
-    brows = count // eg.shape[0]
-
     def block(b, carry):
         rows = pl.ds(pl.multiple_of(b * brows, brows), brows)
         lowb = low[rows, :]
-        gate = acc[rows, pl.ds(0, units)] + SCALE * jnp.dot(lowb, eg[b], preferred_element_type=F32)
-        up = acc[rows, pl.ds(units, units)] + SCALE * jnp.dot(lowb, eu[b], preferred_element_type=F32)
+        of_gate, of_up = expands[0, adapters[b]], expands[1, adapters[b]]
+        blank = jnp.zeros_like(of_gate)
+        of_gate, of_up = jnp.concatenate([of_gate, blank], axis=0), jnp.concatenate([blank, of_up], axis=0)
+        gate = acc[rows, pl.ds(0, units)] + SCALE * jnp.dot(lowb, of_gate, preferred_element_type=F32)
+        up = acc[rows, pl.ds(units, units)] + SCALE * jnp.dot(lowb, of_up, preferred_element_type=F32)
         hidden[rows, :] = (gate / (1.0 + jnp.exp(-gate)) * up).astype(BF16)
         return carry
 
-    lax.fori_loop(0, eg.shape[0], block, 0)
+    lax.fori_loop(0, blocks, block, 0)
     totals.drain()
     for k in range(1, half + 1):
         for way in (0, 1):
@@ -225,7 +248,7 @@
 
 
 def down_kernel(
-    n, hidden, wd, first, expand, live, out,
+    n, adapters, live, hidden, wd, first, expand, out,
     wbuf, own, sib_out, sib_in, chain_out, chain_in, part, arrived, low,
     w_sem, ring_send, ring_recv, sib_send, sib_recv, s1, r1, s2, r2,
 ):
@@ -233,7 +256,7 @@
     half, chips, core = ring.half, ring.chips, ring.core
     count, width = out.shape
     hrows = count // 2
-    blocks = first.shape[0]
+    blocks = adapters.shape[0]
     brows = count // blocks
     offsets = [half]
     for k in range(half - 1, 0, -1):
@@ -300,7 +323,8 @@
 
     def shrink(b, carry):
         rows = pl.ds(pl.multiple_of(b * brows, brows), brows)
-        part[rows, :] = jnp.dot(hidden[rows, :], first[b], preferred_element_type=F32)
+        factor = first[adapters[b]]
+        part[rows, :] = across(hidden[rows, :], jnp.concatenate([factor, jnp.zeros_like(factor)], axis=0))
         return carry
 
     lax.fori_loop(0, blocks, shrink, 0)
@@ -334,8 +358,11 @@
             rows = pl.ds(pl.multiple_of(b * brows, brows), brows)
             total = own[last, rows, :] + sib_in[last, rows, :].astype(F32)
             total = total + chain_in[0, 0, rows, :].astype(F32) + chain_in[1, 0, rows, :].astype(F32)
-            total = total + SCALE * jnp.dot(low[rows, :], expand[b], preferred_element_type=F32)
-            out[rows, :] = (total * live[rows, :]).astype(BF16)
+            factor = expand[adapters[b]]
+            factor = jnp.concatenate([factor, jnp.zeros_like(factor)], axis=0)
+            total = total + SCALE * jnp.dot(low[rows, :], factor, preferred_element_type=F32)
+            active = lax.broadcasted_iota(jnp.int32, total.shape, 0) < live[b]
+            out[rows, :] = jnp.where(active, total, 0.0).astype(BF16)
             return carry
 
         lax.fori_loop(0, blocks // 2, block, 0)
@@ -352,7 +379,7 @@
         to_sibling(slot).wait_send()
 
 
-def fused_gate_up(n, tok, wg, wu, part, eg, eu):
+def fused_gate_up(n, adapters, tok, wg, wu, gs, us, ge, ue):
     count, width = tok.shape
     units = wg.shape[1]
     chips, half = n // 2, n // 4
@@ -360,25 +387,28 @@
     return pl.pallas_call(
         functools.partial(gate_up_kernel, n),
         out_shape=jax.ShapeDtypeStruct((count, units), BF16),
-        in_specs=[pl.BlockSpec(memory_space=pl.ANY)] * 3 + [pl.BlockSpec(memory_space=pltpu.VMEM)] * 3,
+        in_specs=[pl.BlockSpec(memory_space=pltpu.SMEM)] + [pl.BlockSpec(memory_space=pl.ANY)] * 7,
         out_specs=pl.BlockSpec(memory_space=pltpu.VMEM),
         scratch_shapes=[
             pltpu.VMEM((chips, 2, count, width), BF16),
             pltpu.VMEM((chips, 2 * width, 2 * units), BF16),
             pltpu.VMEM((count, 2 * units), F32),
+            pltpu.VMEM((2, *gs.shape), BF16),
+            pltpu.VMEM((2, *ge.shape), BF16),
+            pltpu.VMEM((count, LANES), F32),
             pltpu.VMEM((n, count // n, LANES), F32),
             pltpu.VMEM((count, LANES), BF16),
-            dma, dma((chips, 2)), dma((2, half, 2)), dma((2, half, 2)), dma((chips, 2)), dma((chips, 2)),
+            dma, dma((4,)), dma((chips, 2)), dma((2, half, 2)), dma((2, half, 2)), dma((chips, 2)), dma((chips, 2)),
             dma((n,)), dma((n,)), dma((n,)), dma((n,)),
         ],
         compiler_params=pltpu.CompilerParams(
             collective_id=0, has_side_effects=True, vmem_limit_bytes=56 * 2**20
         ),
         name="gather_gate_up",
-    )(tok, wg, wu, part, eg, eu)
-
-
-def fused_down(n, hidden, wd, first, expand, live):
+    )(adapters, tok, wg, wu, gs, us, ge, ue)
+
+
+def fused_down(n, adapters, live, hidden, wd, first, expand):
     count, units = hidden.shape
     width = expand.shape[2]
     chips, half = n // 2, n // 4
@@ -386,8 +416,9 @@
     return pl.pallas_call(
         functools.partial(down_kernel, n),
         out_shape=jax.ShapeDtypeStruct((count, width), BF16),
-        in_specs=[pl.BlockSpec(memory_space=pltpu.VMEM), pl.BlockSpec(memory_space=pl.ANY)]
-        + [pl.BlockSpec(memory_space=pltpu.VMEM)] * 3,
+        in_specs=[pl.BlockSpec(memory_space=pltpu.SMEM)] * 2
+        + [pl.BlockSpec(memory_space=pltpu.VMEM), pl.BlockSpec(memory_space=pl.ANY)]
+        + [pl.BlockSpec(memory_space=pltpu.VMEM)] * 2,
         out_specs=pl.BlockSpec(memory_space=pltpu.VMEM),
         scratch_shapes=[
             pltpu.VMEM((chips, 2, units, width), BF16),
@@ -406,31 +437,20 @@
             collective_id=1, has_side_effects=True, vmem_limit_bytes=56 * 2**20
         ),
         name="down_scatter",
-    )(hidden, wd, first, expand, live)
+    )(adapters, live, hidden, wd, first, expand)
 
 
 def kernel_local(
     n, tokens, gate_weight, up_weight, down_weight, gate_shrink, gate_expand, up_shrink, up_expand,
     down_first_factor, down_expand, block_adapter, live_slot_count,
 ):
-    count, width = tokens.shape
-    blocks = block_adapter.shape[0]
-    brows = count // blocks
-    rank = gate_shrink.shape[2]
-    held = LANES - rank
-    shrink = jnp.concatenate([gate_shrink[block_adapter], up_shrink[block_adapter]], axis=2)
-    part = jnp.einsum(
-        "btd,bdr->btr", tokens.reshape(blocks, brows, width), shrink, preferred_element_type=F32
-    ).reshape(count, 2 * rank)
-    below, above = ((0, 0), (0, held), (0, 0)), ((0, 0), (held, 0), (0, 0))
-    eg = jnp.pad(gate_expand[block_adapter], below)
-    eu = jnp.pad(up_expand[block_adapter], above)
-    first = jnp.pad(down_first_factor[block_adapter], ((0, 0), (0, 0), (0, held)))
-    expand = jnp.pad(down_expand[block_adapter], below)
-    active = lax.broadcasted_iota(jnp.int32, (blocks, brows), 1) < live_slot_count[:, None]
-    live = active.reshape(count, 1).astype(F32)
-    hidden = fused_gate_up(n, tokens, gate_weight, up_weight, part, eg, eu)
-    return fused_down(n, hidden, down_weight, first, expand, live)
+    def turned(table):
+        return jnp.swapaxes(table, 1, 2)
+
+    hidden = fused_gate_up(
+        n, block_adapter, tokens, gate_weight, up_weight, turned(gate_shrink), turned(up_shrink), gate_expand, up_expand
+    )
+    return fused_down(n, block_adapter, live_slot_count, hidden, down_weight, turned(down_first_factor), down_expand)
 
 
 def fits(n, tokens, gate_weight, gate_shrink, block_adapter):

time: 156 us -> 135 us (0.87)
  local copies, waits for them, and re-layouts: 17.5 us -> 1.87 us
  matrix products: 2.46 us -> 0 us
  Pallas kernels: 134 us -> 132 us
    gather x9 -> x0, local copies, waits for them, and re-layouts: 7.48 us -> none  [the longest x2 2.36 us: kernel_local(): down_first_factor[block_adapter]]
    pad x4 -> x0, local copies, waits for them, and re-layouts: 7.25 us -> none  [the longest x1 3.22 us: kernel_local(): jnp.pad(down_first_factor[block_adapter], ((0, 0), (0, 0), (0, held)))]
    dot_general x1 -> x0, matrix products: 2.46 us -> none  [kernel_local(): jnp.einsum('btd,bdr->btr', tokens.reshape(blocks, brows, width), shrink,...]
where the time goes in v2:
time: 135 us; the launch traced here: 134 us
  Pallas kernels  132 us (98%)
  local copies, waits for them, and re-layouts  1.87 us (1%)
    pallas_call x1, Pallas kernels, fused_gate_up(): pl.pallas_call(functools.partial(gate_up_kernel, n), out_shape=jax.ShapeD...  73.9 us
    pallas_call x1, Pallas kernels, fused_down(): pl.pallas_call(functools.partial(down_kernel, n), out_shape=jax.ShapeDtyp...  58.5 us

profile of v2, /device:TPU:0, one launch (start us, length us, event | category | flops | bytes accessed | tf_op | source)
XLA Modules:
  0.0 134.3 jit_solution(10004232677584248229)
XLA Ops:
  0.0 73.9 %gather_gate_up.1.hidden = bf16[512,896]{1,0:T(8,128)(2,1)} custom-call(s32[8]{0:T(128)} %adapters.3, bf16[512,512]{1,0:T(8,128)(2,1)} %tok.1, bf16[8192,896]{1,0:T(8,128)(2,1)} %wg.1, bf16[8192,896]{1,0:T(8,128)(2,1)} %wu.1, bf16[8,64,512]{2,1,0:T(8,128)(2,1)} %bitcast.4, bf16[8,64,512]{2,1,0:T(8,128)(2,1)} %bitcast.5, bf16[8,64,896]{2,1,0:T(8,128)(2,1)} %ge.1, ...), custom_call_target="tpu_custom_call" | custom-call | tf_op jit(solution)/shard_map/gather_gate_up/pallas_call | solution.py:387
  74.0 58.5 %down_scatter.1 = bf16[512,512]{1,0:T(8,128)(2,1)} custom-call(s32[8]{0:T(128)} %adapters.3, s32[8]{0:T(128)} %live.1, bf16[512,896]{1,0:T(8,128)(2,1)} %gather_gate_up.1.hidden, bf16[896,8192]{1,0:T(8,128)(2,1)} %wd.1, bf16[8,64,896]{2,1,0:T(8,128)(2,1)} %bitcast.3, bf16[8,64,512]{2,1,0:T(8,128)(2,1)} %expand.1), custom_call_target="tpu_custom_call" | custom-call | tf_op jit(solution)/shard_map/down_scatter/pallas_call | solution.py:416
  132.5 1.9 %copy.14 = bf16[512,512]{1,0:T(8,128)(2,1)} copy(bf16[512,512]{1,0:T(8,128)(2,1)} %down_scatter.1) | data formatting | bytes 1048576

commit v3 on v2

--- a/solution.py
+++ b/solution.py
@@ -30,8 +30,8 @@
         far = place + row * (2 * self.side - 1 - 2 * place)
         return far * 2 + row
 
-    def peer(self, step):
-        return lax.rem(self.me + step, self.n)
+    def peer_chip(self, step):
+        return lax.rem(self.chip + step, self.chips)
 
     def sends(self, way, k, h):
         return k < self.half or (k == self.half and h == way)
@@ -40,12 +40,16 @@
 def greet(ring):
     barrier = pltpu.get_barrier_semaphore()
 
+    def greet_device(device):
+        pl.semaphore_signal(barrier, inc=1, device_id={"tensor": device}, device_id_type=pl.DeviceIdType.MESH)
+
     def tell(step, carry):
-        pl.semaphore_signal(barrier, inc=1, device_id={"tensor": ring.peer(step)}, device_id_type=pl.DeviceIdType.MESH)
+        greet_device(ring.peer_chip(step) * 2 + ring.core)
         return carry
 
-    lax.fori_loop(1, ring.n, tell, 0)
-    pl.semaphore_wait(barrier, ring.n - 1)
+    greet_device(ring.sibling)
+    lax.fori_loop(1, ring.chips, tell, 0)
+    pl.semaphore_wait(barrier, ring.chips)
 
 
 def remote(src, dst, send, recv, device):
@@ -60,56 +64,100 @@
 
 
 class Totals:
-    def __init__(self, ring, part, arrived, low, sems):
-        self.ring, self.part, self.arrived, self.low = ring, part, arrived, low
-        self.s1, self.r1, self.s2, self.r2 = sems
-        self.rows = part.shape[0] // ring.n
-
-    def rows_of(self, device):
-        return pl.ds(pl.multiple_of(device * self.rows, self.rows), self.rows)
+    def __init__(self, ring, part, beside, mid, arrived, low, sems):
+        self.ring, self.part, self.beside, self.mid, self.arrived, self.low = ring, part, beside, mid, arrived, low
+        self.s0, self.r0, self.s1, self.r1, self.s2, self.r2 = sems
+        self.held = part.shape[0] // 2
+        self.rows = self.held // ring.chips
+
+    def half_of(self, core):
+        return pl.ds(pl.multiple_of(core * self.held, self.held), self.held)
+
+    def rows_of(self, chip):
+        return pl.ds(pl.multiple_of(chip * self.rows, self.rows), self.rows)
+
+    def low_of(self, chip):
+        return self.low.at[pl.ds(pl.multiple_of(self.ring.core * self.held + chip * self.rows, self.rows), self.rows)]
+
+    def peer(self, step):
+        chip = self.ring.peer_chip(step)
+        return chip, chip * 2 + self.ring.core
+
+    def pairing(self):
+        rows = self.part.at[self.half_of(1 - self.ring.core)]
+        return remote(rows, self.beside, self.s0.at[0], self.r0.at[0], self.ring.sibling)
+
+    def sharing(self, core):
+        rows = self.low.at[self.half_of(core)]
+        return remote(rows, rows, self.s0.at[1], self.r0.at[1], self.ring.sibling)
 
     def first(self, step):
-        peer = self.ring.peer(step)
-        return remote(self.part.at[self.rows_of(peer)], self.arrived.at[step], self.s1.at[step], self.r1.at[step], peer)
+        chip, device = self.peer(step)
+        return remote(self.mid.at[self.rows_of(chip)], self.arrived.at[step], self.s1.at[step], self.r1.at[step], device)
 
     def second(self, step):
-        rows = self.low.at[self.rows_of(self.ring.me)]
-        return remote(rows, rows, self.s2.at[step], self.r2.at[step], self.ring.peer(step))
+        rows = self.low_of(self.ring.chip)
+        return remote(rows, rows, self.s2.at[step], self.r2.at[step], self.peer(step)[1])
 
     def each(self, do):
         def body(step, carry):
             do(step)
             return carry
 
-        lax.fori_loop(1, self.ring.n, body, 0)
+        lax.fori_loop(1, self.ring.chips, body, 0)
+
+    def pair(self):
+        self.pairing().start()
 
     def scatter(self):
+        self.pairing().wait_recv()
+        self.beside[...] = self.beside[...] + self.part[self.half_of(self.ring.core), :]
+        self.mid[...] = self.beside[...].astype(BF16)
         self.each(lambda step: self.first(step).start())
 
     def gather(self):
         self.each(lambda step: self.first(step).wait_recv())
-        total = self.part[self.rows_of(self.ring.me), :]
-        for step in range(1, self.ring.n):
-            total = total + self.arrived[step]
-        self.low[self.rows_of(self.ring.me), :] = total.astype(BF16)
+        total = self.beside[self.rows_of(self.ring.chip), :]
+        for step in range(1, self.ring.chips):
+            total = total + self.arrived[step].astype(F32)
+        start = pl.multiple_of(self.ring.core * self.held + self.ring.chip * self.rows, self.rows)
+        self.low[pl.ds(start, self.rows), :] = total.astype(BF16)
         self.each(lambda step: self.second(step).start())
 
+    def share(self):
+        def wait(step):
+            rows = self.low_of(self.ring.peer_chip(self.ring.chips - step))
+            remote(rows, rows, self.s2.at[step], self.r2.at[step], self.peer(step)[1]).wait_recv()
+
+        self.each(wait)
+        self.sharing(self.ring.core).start()
+
     def finish(self):
-        def wait(step):
-            rows = self.low.at[self.rows_of(self.ring.peer(self.ring.n - step))]
-            remote(rows, rows, self.s2.at[step], self.r2.at[step], self.ring.peer(step)).wait_recv()
-
-        self.each(wait)
+        self.sharing(1 - self.ring.core).wait_recv()
 
     def drain(self):
+        self.pairing().wait_send()
         self.each(lambda step: self.first(step).wait_send())
         self.each(lambda step: self.second(step).wait_send())
+        self.sharing(self.ring.core).wait_send()
+
+    @staticmethod
+    def scratch(rows, chips):
+        dma, held = pltpu.SemaphoreType.DMA, rows // 2
+        refs = [
+            pltpu.VMEM((rows, LANES), F32),
+            pltpu.VMEM((held, LANES), F32),
+            pltpu.VMEM((held, LANES), BF16),
+            pltpu.VMEM((chips, held // chips, LANES), BF16),
+            pltpu.VMEM((rows, LANES), BF16),
+        ]
+        return refs, [dma((2,)), dma((2,))] + [dma((chips,))] * 4
 
 
 def gate_up_kernel(
     n, adapters, tok, wg, wu, gs, us, ge, ue, hidden,
-    gath, wbuf, acc, shrinks, expands, part, arrived, low,
-    tok_sem, table_sem, w_sem, ring_send, ring_recv, sib_send, sib_recv, s1, r1, s2, r2,
+    gath, wbuf, acc, shrinks, expands, part, beside, mid, arrived, low,
+    tok_sem, table_sem, w_sem, ring_send, ring_recv, sib_send, sib_recv, *sems,
 ):
     ring = Ring(n)
     half, chips, core = ring.half, ring.chips, ring.core
@@ -188,7 +236,7 @@
     for slot in range(chips):
         for copy in weight_copies(slot):
             copy.start()
-    totals = Totals(ring, part, arrived, low, (s1, r1, s2, r2))
+    totals = Totals(ring, part, beside, mid, arrived, low, sems)
     greet(ring)
     own.wait()
     for h in (0, 1):
@@ -205,11 +253,12 @@
         return carry
 
     lax.fori_loop(0, blocks, shrink, 0)
+    totals.pair()
     totals.scatter()
     multiply(0)
     relay(1, 0)
+    relay(1, 1)
     totals.gather()
-    relay(1, 1)
     for k in range(2, half + 1):
         if k < half:
             relay(k, 0)
@@ -217,6 +266,7 @@
             relay(k, 1)
             multiply(k - 1)
         else:
+            totals.share()
             multiply(1 - k)
             relay(k, 0)
             relay(k, 1)
@@ -249,8 +299,8 @@
 
 def down_kernel(
     n, adapters, live, hidden, wd, first, expand, out,
-    wbuf, own, sib_out, sib_in, chain_out, chain_in, part, arrived, low,
-    w_sem, ring_send, ring_recv, sib_send, sib_recv, s1, r1, s2, r2,
+    wbuf, own, sib_out, sib_in, chain_out, chain_in, part, beside, mid, arrived, low,
+    w_sem, ring_send, ring_recv, sib_send, sib_recv, *sems,
 ):
     ring = Ring(n)
     half, chips, core = ring.half, ring.chips, ring.core
@@ -323,13 +373,17 @@
 
     def shrink(b, carry):
         rows = pl.ds(pl.multiple_of(b * brows, brows), brows)
-        factor = first[adapters[b]]
-        part[rows, :] = across(hidden[rows, :], jnp.concatenate([factor, jnp.zeros_like(factor)], axis=0))
+        lower = pl.ds(pl.multiple_of(hrows + b * brows, brows), brows)
+        factor, other = first[adapters[b]], first[adapters[b + blocks // 2]]
+        blank = jnp.zeros_like(factor)
+        left = across(hidden[rows, :], jnp.concatenate([factor, blank], axis=0))
+        part[rows, :] = left + across(hidden[lower, :], jnp.concatenate([blank, other], axis=0))
         return carry
 
-    lax.fori_loop(0, blocks, shrink, 0)
-    totals = Totals(ring, part, arrived, low, (s1, r1, s2, r2))
+    lax.fori_loop(0, blocks // 2, shrink, 0)
+    totals = Totals(ring, part, beside, mid, arrived, low, sems)
     greet(ring)
+    totals.pair()
     multiply(half)
     totals.scatter()
     await_sibling(half)
@@ -345,6 +399,7 @@
         if k == 1:
             multiply(0)
         send(k, 1)
+    totals.share()
     totals.finish()
     await_sibling(0)
     last = slot_of[0]
@@ -359,8 +414,10 @@
             total = own[last, rows, :] + sib_in[last, rows, :].astype(F32)
             total = total + chain_in[0, 0, rows, :].astype(F32) + chain_in[1, 0, rows, :].astype(F32)
             factor = expand[adapters[b]]
-            factor = jnp.concatenate([factor, jnp.zeros_like(factor)], axis=0)
-            total = total + SCALE * jnp.dot(low[rows, :], factor, preferred_element_type=F32)
+            pieces = [factor, jnp.zeros_like(factor)]
+            factor = jnp.concatenate(pieces if h == 0 else pieces[::-1], axis=0)
+            packed = pl.ds(pl.multiple_of(i * brows, brows), brows)
+            total = total + SCALE * jnp.dot(low[packed, :], factor, preferred_element_type=F32)
             active = lax.broadcasted_iota(jnp.int32, total.shape, 0) < live[b]
             out[rows, :] = jnp.where(active, total, 0.0).astype(BF16)
             return carry
@@ -384,6 +441,7 @@
     units = wg.shape[1]
     chips, half = n // 2, n // 4
     dma = pltpu.SemaphoreType.DMA
+    refs, sems = Totals.scratch(count, chips)
     return pl.pallas_call(
         functools.partial(gate_up_kernel, n),
         out_shape=jax.ShapeDtypeStruct((count, units), BF16),
@@ -395,11 +453,9 @@
             pltpu.VMEM((count, 2 * units), F32),
             pltpu.VMEM((2, *gs.shape), BF16),
             pltpu.VMEM((2, *ge.shape), BF16),
-            pltpu.VMEM((count, LANES), F32),
-            pltpu.VMEM((n, count // n, LANES), F32),
-            pltpu.VMEM((count, LANES), BF16),
+            *refs,
             dma, dma((4,)), dma((chips, 2)), dma((2, half, 2)), dma((2, half, 2)), dma((chips, 2)), dma((chips, 2)),
-            dma((n,)), dma((n,)), dma((n,)), dma((n,)),
+            *sems,
         ],
         compiler_params=pltpu.CompilerParams(
             collective_id=0, has_side_effects=True, vmem_limit_bytes=56 * 2**20
@@ -413,6 +469,7 @@
     width = expand.shape[2]
     chips, half = n // 2, n // 4
     dma = pltpu.SemaphoreType.DMA
+    refs, sems = Totals.scratch(count // 2, chips)
     return pl.pallas_call(
         functools.partial(down_kernel, n),
         out_shape=jax.ShapeDtypeStruct((count, width), BF16),
@@ -427,11 +484,9 @@
             pltpu.VMEM((chips, count, width), BF16),
             pltpu.VMEM((2, half, count, width), BF16),
             pltpu.VMEM((2, half, count, width), BF16),
-            pltpu.VMEM((count, LANES), F32),
-            pltpu.VMEM((n, count // n, LANES), F32),
-            pltpu.VMEM((count, LANES), BF16),
+            *refs,
             dma((chips, 2)), dma((2, half, 2)), dma((2, half, 2)), dma((chips,)), dma((chips,)),
-            dma((n,)), dma((n,)), dma((n,)), dma((n,)),
+            *sems,
         ],
         compiler_params=pltpu.CompilerParams(
             collective_id=1, has_side_effects=True, vmem_limit_bytes=56 * 2**20
@@ -457,7 +512,7 @@
     count, width = tokens.shape
     units = gate_weight.shape[1]
     return (
-        n % 4 == 0 and n >= 8 and count % (16 * n) == 0 and width % LANES == 0 and units % LANES == 0
+        n % 4 == 0 and n >= 8 and count % (32 * n) == 0 and width % LANES == 0 and units % LANES == 0
         and 2 * gate_shrink.shape[2] == LANES and block_adapter.shape[0] % 2 == 0
         and (count // block_adapter.shape[0]) % 16 == 0
     )

time: 135 us -> 124 us (0.919)
  Pallas kernels: 132 us -> 122 us
    pallas_call x1, Pallas kernels: 73.9 us -> 67.9 us  [fused_gate_up(): pl.pallas_call(functools.partial(gate_up_kernel, n), out_shape=jax.ShapeD...]
    pallas_call x1, Pallas kernels: 58.5 us -> 54 us  [fused_down(): pl.pallas_call(functools.partial(down_kernel, n), out_shape=jax.ShapeDtyp...]
where the time goes in v3:
time: 124 us
  Pallas kernels  122 us (98%)
  local copies, waits for them, and re-layouts  1.87 us (2%)
    pallas_call x1, Pallas kernels, fused_gate_up(): pl.pallas_call(functools.partial(gate_up_kernel, n), out_shape=jax.ShapeD...  67.9 us
    pallas_call x1, Pallas kernels, fused_down(): pl.pallas_call(functools.partial(down_kernel, n), out_shape=jax.ShapeDtyp...  54 us

profile of v3, /device:TPU:0, one launch (start us, length us, event | category | flops | bytes accessed | tf_op | source)
XLA Modules:
  0.0 123.8 jit_solution(2536394327158201575)
XLA Ops:
  0.0 67.9 %gather_gate_up.1.hidden = bf16[512,896]{1,0:T(8,128)(2,1)} custom-call(s32[8]{0:T(128)} %adapters.3, bf16[512,512]{1,0:T(8,128)(2,1)} %tok.1, bf16[8192,896]{1,0:T(8,128)(2,1)} %wg.1, bf16[8192,896]{1,0:T(8,128)(2,1)} %wu.1, bf16[8,64,512]{2,1,0:T(8,128)(2,1)} %bitcast.4, bf16[8,64,512]{2,1,0:T(8,128)(2,1)} %bitcast.5, bf16[8,64,896]{2,1,0:T(8,128)(2,1)} %ge.1, ...), custom_call_target="tpu_custom_call" | custom-call | tf_op jit(solution)/shard_map/gather_gate_up/pallas_call | solution.py:445
  67.9 54.0 %down_scatter.1 = bf16[512,512]{1,0:T(8,128)(2,1)} custom-call(s32[8]{0:T(128)} %adapters.3, s32[8]{0:T(128)} %live.1, bf16[512,896]{1,0:T(8,128)(2,1)} %gather_gate_up.1.hidden, bf16[896,8192]{1,0:T(8,128)(2,1)} %wd.1, bf16[8,64,896]{2,1,0:T(8,128)(2,1)} %bitcast.3, bf16[8,64,512]{2,1,0:T(8,128)(2,1)} %expand.1), custom_call_target="tpu_custom_call" | custom-call | tf_op jit(solution)/shard_map/down_scatter/pallas_call | solution.py:473
  121.9 1.9 %copy.14 = bf16[512,512]{1,0:T(8,128)(2,1)} copy(bf16[512,512]{1,0:T(8,128)(2,1)} %down_scatter.1) | data formatting | bytes 1048576
